TPU v7x, 128 devices: a whole 4x4x4 slice. The times are simulated.
128 devices in a mesh: group: 8 (over z, core), member: 16 (over x, y).
Axes of the slice: x: 4, y: 4, z: 4, core: 2. Of those that a mesh axis runs over, the one named last changes fastest.
Arguments:
- query_feat: bfloat16 [16384, 4096], P(('group', 'member'))
- code_feat: bfloat16 [16384, 4096], P(('group', 'member'))
- projection: bfloat16 [4096, 1024], replicated
- hard_ids: int32 [128, 16], P(('group', 'member')), may hold values from 0 to 255, as said below
- loss_weight: float32 [16384], P(('group', 'member')), may hold values from 1 to 4
Outputs:
- query_grad: bfloat16 [16384, 4096], P(('group', 'member'))
- code_grad: bfloat16 [16384, 4096], P(('group', 'member'))
- projection_grad: float32 [4096, 1024], P(('group', 'member'))
Inputs may be any that keep to these rules, and one draw needn't show every extreme that they name: `hard_ids`: entry (owner device g * 16 + m) * 2 + slot names code rows of that device. A row names 16 different blocks, none of its own group; at most 4 of them lie in one group, and exactly 4 in some group of every row.
All inputs are finite; a program needn't handle non-finite values.
Results may differ from a plain program's by a relative error of at most 0.02.
Values may be sent and summed in bfloat16 or wider, within the bound.
A program may use at most 128 MiB of HBM per device.

v0:
```python
import jax
import jax.numpy as jnp
from jax import lax
from jax.sharding import PartitionSpec as P

CB = 64
inverse_temp = 120.0
epsilon = 1e-06


def embed(features, projection):
    values = jnp.dot(features, projection, preferred_element_type=jnp.float32)
    inverse = lax.rsqrt(jnp.sum(values * values, axis=1) + epsilon)
    unit_vec = values * inverse[:, None]
    return (unit_vec, inverse, unit_vec.astype(jnp.bfloat16))


def norm_back(upstream, unit_vec, inverse):
    inner_prod = jnp.sum(unit_vec * upstream, axis=1, keepdims=True)
    return (inverse[:, None] * (upstream - unit_vec * inner_prod)).astype(jnp.bfloat16)


def body(query_feat, code_feat, projection, hard_ids, loss_weight):
    groups = lax.axis_size("group")
    members = lax.axis_size("member")
    member_index = lax.axis_index("member")
    queries_dev = query_feat.shape[0]
    emb_width = projection.shape[1]
    count_hard = hard_ids.shape[1]
    slot_count = queries_dev // CB
    per_group = members * slot_count
    capacity = 2 * count_hard // groups
    q_unit, q_inv, q_emb = embed(query_feat, projection)
    c_unit, c_inv, c_emb = embed(code_feat, projection)
    group_codes = lax.all_gather(c_emb, "member", axis=0, tiled=True)
    code_blocks = group_codes.reshape(per_group, CB, emb_width)
    wanted = hard_ids[0]
    owner_group = wanted // per_group
    local_block = wanted % per_group
    request_order = jnp.arange(count_hard, dtype=jnp.int32)
    same_group = (owner_group[:, None] == owner_group[None, :]) & (
        request_order[None, :] < request_order[:, None]
    )
    slot_place = jnp.sum(same_group.astype(jnp.int32), axis=1)
    pick_group = (owner_group[:, None] == jnp.arange(groups, dtype=jnp.int32)[None, :]).astype(
        jnp.int32
    )
    pick_place = (slot_place[:, None] == jnp.arange(capacity, dtype=jnp.int32)[None, :]).astype(
        jnp.int32
    )
    request_table = (
        jnp.sum(
            pick_group[:, :, None] * (pick_place * (local_block + 1)[:, None])[:, None, :], axis=0
        )
        - 1
    )
    asked_blocks = lax.all_to_all(request_table, "group", split_axis=0, concat_axis=0, tiled=True)
    asked_valid = asked_blocks >= 0
    picked = (
        code_blocks[jnp.clip(asked_blocks, 0, per_group - 1)]
        * asked_valid.astype(jnp.bfloat16)[:, :, None, None]
    )
    group_scores = inverse_temp * jnp.einsum(
        "qe,ke->qk", q_emb, group_codes, preferred_element_type=jnp.float32
    )
    offsets = jnp.arange(queries_dev, dtype=jnp.int32)
    columns = jnp.arange(members * queries_dev, dtype=jnp.int32)
    positive = (columns[None, :] == (member_index * queries_dev + offsets)[:, None]).astype(
        jnp.float32
    )
    factor = loss_weight * inverse_temp
    fetched = lax.all_to_all(picked, "group", split_axis=0, concat_axis=0, tiled=True).reshape(
        groups * capacity * CB, emb_width
    )
    table_valid = jnp.broadcast_to(
        (request_table >= 0)[:, :, None], (groups, capacity, CB)
    ).reshape(-1)
    hard_scores = jnp.where(
        table_valid[None, :],
        inverse_temp * jnp.einsum("qe,ke->qk", q_emb, fetched, preferred_element_type=jnp.float32),
        -jnp.inf,
    )
    row_max = jnp.maximum(jnp.max(group_scores, axis=1), jnp.max(hard_scores, axis=1))
    row_sum = jnp.sum(jnp.exp(group_scores - row_max[:, None]), axis=1) + jnp.sum(
        jnp.exp(hard_scores - row_max[:, None]), axis=1
    )
    log_total = row_max + jnp.log(row_sum)
    grad_hard = (factor[:, None] * jnp.exp(hard_scores - log_total[:, None])).astype(jnp.bfloat16)
    hard_delta = jnp.einsum("qk,ke->qe", grad_hard, fetched, preferred_element_type=jnp.float32)
    outgoing = jnp.einsum("qk,qe->ke", grad_hard, q_emb, preferred_element_type=jnp.float32).astype(
        jnp.bfloat16
    )
    returned = lax.all_to_all(
        outgoing.reshape(groups, capacity, CB, emb_width),
        "group",
        split_axis=0,
        concat_axis=0,
        tiled=True,
    )
    grad_group = (factor[:, None] * (jnp.exp(group_scores - log_total[:, None]) - positive)).astype(
        jnp.bfloat16
    )
    query_delta = (
        jnp.einsum("qk,ke->qe", grad_group, group_codes, preferred_element_type=jnp.float32)
        + hard_delta
    )
    hit_table = (
        asked_blocks.reshape(-1)[:, None] == jnp.arange(per_group, dtype=jnp.int32)[None, :]
    ).astype(jnp.bfloat16)
    hard_sum = jnp.einsum(
        "rj,rx->jx",
        hit_table,
        returned.reshape(groups * capacity, CB * emb_width),
        preferred_element_type=jnp.float32,
    )
    code_terms = jnp.einsum(
        "qk,qe->ke", grad_group, q_emb, preferred_element_type=jnp.float32
    ) + hard_sum.reshape(members * queries_dev, emb_width)
    code_delta = lax.psum_scatter(
        code_terms.astype(jnp.bfloat16), "member", scatter_dimension=0, tiled=True
    ).astype(jnp.float32)
    dz_query = norm_back(query_delta, q_unit, q_inv)
    dz_code = norm_back(code_delta, c_unit, c_inv)
    query_grad = jnp.einsum(
        "qe,de->qd", dz_query, projection, preferred_element_type=jnp.float32
    ).astype(jnp.bfloat16)
    code_grad = jnp.einsum(
        "qe,de->qd", dz_code, projection, preferred_element_type=jnp.float32
    ).astype(jnp.bfloat16)
    projection_grad = lax.psum_scatter(
        jnp.einsum("qd,qe->de", query_feat, dz_query, preferred_element_type=jnp.float32)
        + jnp.einsum("qd,qe->de", code_feat, dz_code, preferred_element_type=jnp.float32),
        ("group", "member"),
        scatter_dimension=0,
        tiled=True,
    )
    return (query_grad, code_grad, projection_grad)


def solution(mesh):
    return jax.shard_map(
        body,
        mesh=mesh,
        in_specs=(
            P(("group", "member"), None),
            P(("group", "member"), None),
            P(),
            P(("group", "member"), None),
            P(("group", "member")),
        ),
        out_specs=(
            P(("group", "member"), None),
            P(("group", "member"), None),
            P(("group", "member"), None),
        ),
        check_vma=False,
    )
```

profile of v0, /device:TPU:0, one launch (start us, length us, event | category | flops | bytes accessed | tf_op | source)
XLA Modules:
  0.0 1007.8 jit_solution(13707422682799377687)
XLA Ops:
  7.2 5.1 multiply_reduce_fusion.1
  14.5 10.5 %all_to_all.16 = s32[8,1,4]{2,1,0:T(1,128)S(1)} all-to-all(s32[8,1,4]{2,1,0:T(1,128)S(1)} %copy.33), channel_id=1, replica_groups=mesh['group'=8,'member'=16] {'group'}, dimensions={0} | all-to-all | bytes 256 | tf_op jit(solution)/shard_map/all_to_all | solution.py:57
  25.3 42.7 %all-gather.2.cloned.1.call-done = bf16[2048,1024]{1,0:T(8,128)(2,1)} async-done(((bf16[128,1024]{1,0:T(8,128)(2,1)}), bf16[2048,1024]{1,0:T(8,128)(2,1)}) %all-gather.2.cloned.1.call-update) | async-done | bytes 4194320 | tf_op jit(solution)/shard_map/all_gather | solution.py:35
  68.0 5.0 gather_fusion
  73.0 4.5 broadcast_multiply_fusion
  77.4 4.6 all-to-all-start.1
  82.3 4.9 multiply_reduce_fusion.2
  89.6 42.0 %all-to-all-done.1 = bf16[8,4,64,1024]{3,2,1,0:T(8,128)(2,1)} async-done(((bf16[8,4,64,1024]{3,2,1,0:T(8,128)(2,1)}), bf16[8,4,64,1024]{3,2,1,0:T(8,128)(2,1)}, u32[]{:S(2)}, u32[]{:S(2)}) %all-to-all-start.1) | async-done | bytes 4194336 | tf_op jit(solution)/shard_map/all_to_all | solution.py:72
  131.6 3.8 fusion.14
  135.9 3.4 convolution_convert_fusion.2
  139.2 4.5 all-to-all-start.2
  145.3 48.2 %all-to-all-done.2 = bf16[8,4,64,1024]{3,2,1,0:T(8,128)(2,1)} async-done(((bf16[8,4,64,1024]{3,2,1,0:T(8,128)(2,1)}), bf16[8,4,64,1024]{3,2,1,0:T(8,128)(2,1)}, u32[]{:S(2)}, u32[]{:S(2)}) %all-to-all-start.2) | async-done | bytes 4194336 | tf_op jit(solution)/shard_map/all_to_all | solution.py:93
  193.5 4.5 copy.41
  198.0 4.6 fusion.4
  202.5 7.5 reshape.206
  210.0 6.8 add_convert_fusion
  217.1 3.1 fusion.12
  223.6 8.1 fusion.15
  231.7 60.6 %reduce-scatter.5.cloned.1.call-done = bf16[128,1024]{1,0:T(8,128)(2,1)} async-done(((bf16[2048,1024]{1,0:T(8,128)(2,1)}), bf16[128,1024]{1,0:T(8,128)(2,1)}) %reduce-scatter.5.cloned.1.call-update) | async-done | bytes 262160 | tf_op jit(solution)/shard_map/reduce_scatter | solution.py:119
  294.6 13.9 %add_bitcast_fusion = f32[4096,1024]{0,1:T(8,128)} fusion(f32[1024,4096]{1,0:T(8,128)} %fusion.15, bf16[128,1024]{1,0:T(8,128)(2,1)S(1)} %fusion.3, bf16[128,4096]{1,0:T(8,128)(2,1)S(1)} %copy-done.7), kind=kOutput, calls=%fused_computation.1 | convolution fusion | flops 1077936128 | bytes 34865152 | tf_op jit(solution)/shard_map/qd,qe->de/dot_general | solution.py:132
  308.4 17.5 %copy.39 = f32[4096,1024]{1,0:T(8,128)} copy(f32[4096,1024]{0,1:T(8,128)} %add_bitcast_fusion) | data formatting | bytes 33554432
  325.9 7.3 convolution_convert_fusion.1
  333.2 7.3 convolution_convert_fusion
  340.6 660.7 %reduce-scatter.7.cloned.1.call-done = f32[32,1024]{1,0:T(8,128)} async-done(((f32[4096,1024]{1,0:T(8,128)}), f32[32,1024]{1,0:T(8,128)}) %reduce-scatter.7.cloned.1.call-update) | async-done | bytes 131088
  (61 shorter events, 13.0 us)
Async XLA Ops:
  7.2 75.1 %copy-start = (bf16[128,4096]{1,0:T(8,128)(2,1)S(1)}, bf16[128,4096]{1,0:T(8,128)(2,1)}, u32[]{:S(2)}) copy-start(bf16[128,4096]{1,0:T(8,128)(2,1)} %param.5) | copy-start | bytes 3145732
  7.2 6.8 copy-start.9
  7.2 60.8 %all-gather.2.cloned.1.call-start = ((), (), s32[]{:S(2)}) async-start(), calls=%async_computation.5 | async-start | bytes 4456448 | tf_op jit(solution)/shard_map/all_gather | solution.py:35
  12.4 0.8 copy-start.3
  77.4 54.2 %all-to-all-start.1 = ((bf16[8,4,64,1024]{3,2,1,0:T(8,128)(2,1)}), bf16[8,4,64,1024]{3,2,1,0:T(8,128)(2,1)}, u32[]{:S(2)}, u32[]{:S(2)}) async-start(bf16[8,4,64,1024]{3,2,1,0:T(8,128)(2,1)} %broadcast_multiply_fusion), calls=%async_computation.1 | async-start | bytes 8388608 | tf_op jit(solution)/shard_map/all_to_all | solution.py:72
  82.3 4.9 copy-start.8
  82.3 5.8 copy-start.2
  87.1 0.8 copy-start.5
  139.2 54.2 %all-to-all-start.2 = ((bf16[8,4,64,1024]{3,2,1,0:T(8,128)(2,1)}), bf16[8,4,64,1024]{3,2,1,0:T(8,128)(2,1)}, u32[]{:S(2)}, u32[]{:S(2)}) async-start(bf16[8,4,64,1024]{3,2,1,0:T(8,128)(2,1)} %bitcast.58), calls=%async_computation.2 | async-start | bytes 8388608 | tf_op jit(solution)/shard_map/all_to_all | solution.py:93
  143.8 148.5 %reduce-scatter.5.cloned.1.call-start = ((), (), s32[]{:S(2)}) async-start(), calls=%async_computation.6 | async-start | bytes 4456448 | tf_op jit(solution)/shard_map/reduce_scatter | solution.py:119
  216.9 784.4 %reduce-scatter.7.cloned.1.call-start = ((), (), s32[]{:S(2)}) async-start(), calls=%async_computation.7 | async-start | bytes 16908288
  217.1 3.1 copy-start.6
  223.5 68.7 %copy-start.4 = (f32[128,1024]{1,0:T(8,128)S(1)}, f32[128,1024]{1,0:T(8,128)}, u32[]{:S(2)}) copy-start(f32[128,1024]{1,0:T(8,128)} %copy-done.3) | copy-start | bytes 1572868
  223.6 71.0 %copy-start.7 = (bf16[128,4096]{1,0:T(8,128)(2,1)S(1)}, bf16[128,4096]{1,0:T(8,128)(2,1)}, u32[]{:S(2)}) copy-start(bf16[128,4096]{1,0:T(8,128)(2,1)} %param.6) | copy-start | bytes 3145732
  325.9 675.4 %copy-start.1 = (bf16[128,4096]{1,0:T(8,128)(2,1)S(1)}, bf16[128,4096]{1,0:T(8,128)(2,1)}, u32[]{:S(2)}) copy-start(bf16[128,4096]{1,0:T(8,128)(2,1)} %param.5) | copy-start | bytes 3145732
Sparse Core Ops, SparseCore 0:
  14.1 53.8 all-gather.1
  217.0 75.2 reduce-scatter.4
  326.0 675.1 reduce-scatter.6
where the time goes:
time: 1010 us
  waiting for transfers between devices  854 us (85%)
  matrix products  72.9 us (7%)
  local copies, waits for them, and re-layouts  37.3 us (4%)
  between operations  14 us (1%)
  blocking collectives  10.5 us (1%)
    unnamed x4, waiting for transfers between devices  661 us
    reduce_scatter x1, waiting for transfers between devices, body(): lax.psum_scatter(code_terms.astype(jnp.bfloat16), 'member', scatter_dimen...  60.6 us
    all_to_all x1, waiting for transfers between devices, body(): lax.all_to_all(outgoing.reshape(groups, capacity, CB, emb_width), 'group'...  48.2 us
    all_gather x1, waiting for transfers between devices, body(): group_codes = lax.all_gather(c_emb, 'member', axis=0, tiled=True)  42.7 us
    all_to_all x1, waiting for transfers between devices, body(): lax.all_to_all(picked, 'group', split_axis=0, concat_axis=0, tiled=True)  42 us
    unnamed x22, local copies, waits for them, and re-layouts  23.6 us
  transfers between devices with their start and end apart: 5, of which 5 were waited for; matrix products, arithmetic and copies ran while one was open for 4% of the time, Pallas kernels for 0%

commit v1 on v0

--- a/solution.py
+++ b/solution.py
@@ -32,7 +32,9 @@
     capacity = 2 * count_hard // groups
     q_unit, q_inv, q_emb = embed(query_feat, projection)
     c_unit, c_inv, c_emb = embed(code_feat, projection)
-    group_codes = lax.all_gather(c_emb, "member", axis=0, tiled=True)
+    group_codes = jnp.concatenate(
+        lax.all_to_all(jnp.stack([c_emb] * lax.axis_size("member")), "member", 0, 0), axis=0
+    )
     code_blocks = group_codes.reshape(per_group, CB, emb_width)
     wanted = hard_ids[0]
     owner_group = wanted // per_group

time: 1010 us -> 1040 us (1.030)
  waiting for transfers between devices: 854 us -> 873 us
  starting transfers between devices: 9.62 us -> 27 us
  blocking collectives: 10.5 us -> 0 us
    all_to_all x0 -> x2, waiting for transfers between devices: none -> 55.4 us  [the longest x1 55.4 us: body(): lax.all_to_all(jnp.stack([c_emb] * lax.axis_size('member')), 'member', 0, 0)]
    all_gather x1 -> x0, waiting for transfers between devices: 42.7 us -> none  [body(): group_codes = lax.all_gather(c_emb, 'member', axis=0, tiled=True)]
    all_to_all x0 -> x2, starting transfers between devices: none -> 12.5 us  [the longest x1 7.09 us: body(): lax.all_to_all(jnp.stack([c_emb] * lax.axis_size('member')), 'member', 0, 0)]
    all_to_all x1 -> x0, blocking collectives: 10.5 us -> none  [body(): lax.all_to_all(request_table, 'group', split_axis=0, concat_axis=0, tiled...]
    unnamed x4 -> x3, waiting for transfers between devices: 661 us -> 661 us
    unnamed x22 -> x18, local copies, waits for them, and re-layouts: 23.6 us -> 23.5 us
  transfers between devices with their start and end apart: 5 -> 6, of which waited for: 5 -> 5; matrix products, arithmetic and copies ran while one was open for 4% -> 4% of each run, Pallas kernels for 0% -> 0%
where the time goes in v1:
time: 1040 us
  waiting for transfers between devices  873 us (84%)
  matrix products  74.9 us (7%)
  local copies, waits for them, and re-layouts  40.3 us (4%)
  starting transfers between devices  27 us (3%)
  between operations  14.3 us (1%)
    unnamed x3, waiting for transfers between devices  661 us
    reduce_scatter x1, waiting for transfers between devices, body(): lax.psum_scatter(code_terms.astype(jnp.bfloat16), 'member', scatter_dimen...  68 us
    all_to_all x1, waiting for transfers between devices, body(): lax.all_to_all(jnp.stack([c_emb] * lax.axis_size('member')), 'member', 0, 0)  55.4 us
    all_to_all x1, waiting for transfers between devices, body(): lax.all_to_all(outgoing.reshape(groups, capacity, CB, emb_width), 'group'...  48.2 us
    all_to_all x1, waiting for transfers between devices, body(): lax.all_to_all(picked, 'group', split_axis=0, concat_axis=0, tiled=True)  40.2 us
    unnamed x18, local copies, waits for them, and re-layouts  23.5 us
  transfers between devices with their start and end apart: 6, of which 5 were waited for; matrix products, arithmetic and copies ran while one was open for 4% of the time, Pallas kernels for 0%

profile of v1, /device:TPU:0, one launch (start us, length us, event | category | flops | bytes accessed | tf_op | source)
XLA Modules:
  0.0 1039.3 jit_solution(14120673385267480988)
XLA Ops:
  9.6 5.4 all-to-all-start.1
  15.0 5.0 multiply_reduce_fusion.1
  23.5 7.1 all-to-all-start
  30.9 55.4 %all-to-all-done = bf16[16,128,1024]{2,1,0:T(8,128)(2,1)} async-done(((bf16[16,128,1024]{2,1,0:T(8,128)(2,1)}), bf16[16,128,1024]{2,1,0:T(8,128)(2,1)}, u32[]{:S(2)}, u32[]{:S(2)}) %all-to-all-start) | async-done | bytes 4194336 | tf_op jit(solution)/shard_map/all_to_all | solution.py:36
  86.3 5.0 gather_fusion
  91.3 4.5 broadcast_multiply_fusion
  95.7 9.5 all-to-all-start.2
  105.5 4.7 multiply_reduce_fusion.2
  111.0 3.8 fusion.13
  114.8 40.2 %all-to-all-done.2 = bf16[8,4,64,1024]{3,2,1,0:T(8,128)(2,1)} async-done(((bf16[8,4,64,1024]{3,2,1,0:T(8,128)(2,1)}), bf16[8,4,64,1024]{3,2,1,0:T(8,128)(2,1)}, u32[]{:S(2)}, u32[]{:S(2)}) %all-to-all-start.2) | async-done | bytes 4194336 | tf_op jit(solution)/shard_map/all_to_all | solution.py:74
  155.0 3.8 fusion.14
  162.6 4.5 all-to-all-start.3
  168.7 48.2 %all-to-all-done.3 = bf16[8,4,64,1024]{3,2,1,0:T(8,128)(2,1)} async-done(((bf16[8,4,64,1024]{3,2,1,0:T(8,128)(2,1)}), bf16[8,4,64,1024]{3,2,1,0:T(8,128)(2,1)}, u32[]{:S(2)}, u32[]{:S(2)}) %all-to-all-start.3) | async-done | bytes 4194336 | tf_op jit(solution)/shard_map/all_to_all | solution.py:95
  216.8 4.5 copy.41
  221.3 4.6 fusion.4
  225.9 7.5 reshape.208
  233.4 6.8 add_convert_fusion
  246.9 8.1 fusion.15
  255.1 68.0 %reduce-scatter.5.cloned.1.call-done = bf16[128,1024]{1,0:T(8,128)(2,1)} async-done(((bf16[2048,1024]{1,0:T(8,128)(2,1)}), bf16[128,1024]{1,0:T(8,128)(2,1)}) %reduce-scatter.5.cloned.1.call-update) | async-done | bytes 262160 | tf_op jit(solution)/shard_map/reduce_scatter | solution.py:121
  325.4 13.9 %add_bitcast_fusion = f32[4096,1024]{0,1:T(8,128)} fusion(f32[1024,4096]{1,0:T(8,128)} %fusion.15, bf16[128,1024]{1,0:T(8,128)(2,1)S(1)} %fusion.3, bf16[128,4096]{1,0:T(8,128)(2,1)S(1)} %copy-done.6), kind=kOutput, calls=%fused_computation.1 | convolution fusion | flops 1077936128 | bytes 34865152 | tf_op jit(solution)/shard_map/qd,qe->de/dot_general | solution.py:134
  339.2 17.5 %copy.39 = f32[4096,1024]{1,0:T(8,128)} copy(f32[4096,1024]{0,1:T(8,128)} %add_bitcast_fusion) | data formatting | bytes 33554432
  356.7 7.3 convolution_convert_fusion.1
  364.0 7.3 convolution_convert_fusion
  371.4 661.1 %reduce-scatter.7.cloned.1.call-done = f32[32,1024]{1,0:T(8,128)} async-done(((f32[4096,1024]{1,0:T(8,128)}), f32[32,1024]{1,0:T(8,128)}) %reduce-scatter.7.cloned.1.call-update) | async-done | bytes 131088
  (58 shorter events, 21.5 us)
Async XLA Ops:
  7.2 98.3 %copy-start = (bf16[128,4096]{1,0:T(8,128)(2,1)S(1)}, bf16[128,4096]{1,0:T(8,128)(2,1)}, u32[]{:S(2)}) copy-start(bf16[128,4096]{1,0:T(8,128)(2,1)} %param.5) | copy-start | bytes 3145732
  9.6 11.4 %all-to-all-start.1 = ((s32[8,1,4]{2,1,0:T(1,128)}), s32[8,1,4]{2,1,0:T(1,128)S(1)}, u32[]{:S(2)}, u32[]{:S(2)}) async-start(s32[8,1,4]{2,1,0:T(1,128)} %copy.33), calls=%async_computation.1 | async-start | bytes 8192 | tf_op jit(solution)/shard_map/all_to_all | solution.py:59
  20.1 0.8 copy-start.2
  23.5 62.9 %all-to-all-start = ((bf16[16,128,1024]{2,1,0:T(8,128)(2,1)}), bf16[16,128,1024]{2,1,0:T(8,128)(2,1)}, u32[]{:S(2)}, u32[]{:S(2)}) async-start(bf16[16,128,1024]{2,1,0:T(8,128)(2,1)} %stack.2), calls=%async_computation | async-start | bytes 8388608 | tf_op jit(solution)/shard_map/all_to_all | solution.py:36
  95.7 59.3 %all-to-all-start.2 = ((bf16[8,4,64,1024]{3,2,1,0:T(8,128)(2,1)}), bf16[8,4,64,1024]{3,2,1,0:T(8,128)(2,1)}, u32[]{:S(2)}, u32[]{:S(2)}) async-start(bf16[8,4,64,1024]{3,2,1,0:T(8,128)(2,1)} %broadcast_multiply_fusion), calls=%async_computation.2 | async-start | bytes 8388608 | tf_op jit(solution)/shard_map/all_to_all | solution.py:74
  105.5 4.7 copy-start.7
  110.2 0.8 copy-start.4
  162.6 54.2 %all-to-all-start.3 = ((bf16[8,4,64,1024]{3,2,1,0:T(8,128)(2,1)}), bf16[8,4,64,1024]{3,2,1,0:T(8,128)(2,1)}, u32[]{:S(2)}, u32[]{:S(2)}) async-start(bf16[8,4,64,1024]{3,2,1,0:T(8,128)(2,1)} %bitcast.58), calls=%async_computation.3 | async-start | bytes 8388608 | tf_op jit(solution)/shard_map/all_to_all | solution.py:95
  167.2 155.9 %reduce-scatter.5.cloned.1.call-start = ((), (), s32[]{:S(2)}) async-start(), calls=%async_computation.6 | async-start | bytes 4456448 | tf_op jit(solution)/shard_map/reduce_scatter | solution.py:121
  240.2 792.3 %reduce-scatter.7.cloned.1.call-start = ((), (), s32[]{:S(2)}) async-start(), calls=%async_computation.7 | async-start | bytes 16908288
  240.5 3.1 copy-start.5
  246.9 76.1 %copy-start.3 = (f32[128,1024]{1,0:T(8,128)S(1)}, f32[128,1024]{1,0:T(8,128)}, u32[]{:S(2)}) copy-start(f32[128,1024]{1,0:T(8,128)} %copy-done.2) | copy-start | bytes 1572868
  246.9 78.4 %copy-start.6 = (bf16[128,4096]{1,0:T(8,128)(2,1)S(1)}, bf16[128,4096]{1,0:T(8,128)(2,1)}, u32[]{:S(2)}) copy-start(bf16[128,4096]{1,0:T(8,128)(2,1)} %param.6) | copy-start | bytes 3145732
  356.7 675.8 %copy-start.1 = (bf16[128,4096]{1,0:T(8,128)(2,1)S(1)}, bf16[128,4096]{1,0:T(8,128)(2,1)}, u32[]{:S(2)}) copy-start(bf16[128,4096]{1,0:T(8,128)(2,1)} %param.5) | copy-start | bytes 3145732
Sparse Core Ops, SparseCore 0:
  240.3 82.6 reduce-scatter.4
  356.8 675.6 reduce-scatter.6
